TPU v7x, 1024 devices: a whole 4x4x32 slice. The times are simulated.
1024 devices in a mesh: fsdp: 32 (over z), bal: 32 (over y, x, core).
Axes of the slice: x: 4, y: 4, z: 32, core: 2. Of those that a mesh axis runs over, the one named last changes fastest.
Arguments:
- query_rows: bfloat16 [1024, 256, 1024], P('fsdp', 'bal'), may hold values from -40 to 40
- key_rows: bfloat16 [1024, 256, 1024], P('fsdp', 'bal'), may hold values from -40 to 40
- value_rows: bfloat16 [1024, 256, 1024], P('fsdp', 'bal'), may hold values from -12 to 12
- cotangent: bfloat16 [1024, 256, 1024], P('fsdp', 'bal'), may hold values from -0.09375 to 0.09375
- out_weight: bfloat16 [1024, 1024], P('fsdp'), may hold values from -0.1875 to 0.1875
- token_counts: int32 [1024, 32], P('fsdp'), may hold values from 0 to 8, as said below
Outputs:
- mixed: bfloat16 [1024, 256, 1024], P('fsdp', 'bal')
- weight_grad: float32 [1024, 1024], P('fsdp')
Inputs may be any that keep to these rules, and one draw needn't show every extreme that they name: `token_counts`: every cell has at least one live gene token over all its ranges.
All inputs are finite; a program needn't handle non-finite values.
Results may differ from a plain program's by a relative error of at most 0.015.
Values may be sent and summed in bfloat16 or wider, within the bound.
A program may use at most 32 MiB of HBM per device.

v0:
```python
import jax
import jax.numpy as jnp
from jax import lax
from jax.sharding import PartitionSpec as P

HEADS = 8
HEAD_DIM = 128


def attend_items(received):
    query_recv, key_recv, value_recv, mask_recv = received
    items = query_recv.shape[1]
    slots = query_recv.shape[2]
    width = query_recv.shape[3]
    shape_heads = (items, slots, HEADS, HEAD_DIM)
    query_heads = query_recv.reshape(shape_heads)
    key_heads = key_recv.reshape(shape_heads)
    value_heads = value_recv.reshape(shape_heads)
    live = mask_recv.reshape(items, slots) > 0.5
    scores = jnp.einsum(
        "cqhd,ckhd->chqk", query_heads, key_heads, preferred_element_type=jnp.float32
    ) * HEAD_DIM ** (-0.5)
    scores = jnp.where(live[:, None, None, :], scores, -1e30)
    peak = jnp.max(scores, axis=-1, keepdims=True)
    expo = jnp.exp(scores - peak)
    probs = (expo / jnp.sum(expo, axis=-1, keepdims=True)).astype(jnp.bfloat16)
    attended = jnp.einsum("chqk,ckhd->cqhd", probs, value_heads, preferred_element_type=jnp.float32)
    attended = jnp.where(live[:, :, None, None], attended, 0.0)
    attended = attended.astype(jnp.bfloat16).reshape(1, items, slots, width)
    return lax.all_to_all(attended, "bal", split_axis=2, concat_axis=0, tiled=True)


def local(query_rows, key_rows, value_rows, cotangent, out_weight, token_counts):
    cells_here, genes_here, width = query_rows.shape
    group_size = lax.axis_size("bal")
    my_index = lax.axis_index("bal")
    per_device = cells_here // group_size
    index_list = jnp.arange(cells_here, dtype=jnp.int32)
    column = lax.dynamic_slice_in_dim(token_counts, my_index, 1, 1)
    live_home = (jnp.arange(genes_here, dtype=jnp.int32)[None, :] < column).astype(jnp.bfloat16)
    send_shape = (group_size, per_device, genes_here, width)
    query_send = jnp.take(query_rows, index_list, axis=0).reshape(send_shape)
    key_send = jnp.take(key_rows, index_list, axis=0).reshape(send_shape)
    value_send = jnp.take(value_rows, index_list, axis=0).reshape(send_shape)
    mask_send = jnp.take(live_home, index_list, axis=0).reshape(group_size, per_device, genes_here)
    returned = attend_items(
        (
            lax.all_to_all(query_send, "bal", split_axis=0, concat_axis=2, tiled=True),
            lax.all_to_all(key_send, "bal", split_axis=0, concat_axis=2, tiled=True),
            lax.all_to_all(value_send, "bal", split_axis=0, concat_axis=2, tiled=True),
            lax.all_to_all(mask_send, "bal", split_axis=0, concat_axis=2, tiled=True),
        )
    )
    home = jnp.take(returned.reshape(cells_here, genes_here, width), index_list, axis=0)
    attended_flat = home.reshape(cells_here * genes_here, width)
    mixed = lax.dot_general(
        attended_flat,
        lax.all_gather(out_weight, "fsdp", axis=0, tiled=True),
        (((1,), (1,)), ((), ())),
        preferred_element_type=jnp.float32,
    )
    features = cotangent.shape[2]
    mixed = mixed.astype(jnp.bfloat16).reshape(cells_here, genes_here, features)
    grad_flat = cotangent.reshape(cells_here * genes_here, features)
    group_rows = lax.psum_scatter(
        lax.dot_general(
            grad_flat, attended_flat, (((0,), (0,)), ((), ())), preferred_element_type=jnp.float32
        ),
        "fsdp",
        scatter_dimension=0,
        tiled=True,
    )
    weight_grad = lax.psum(group_rows, "bal")
    return (mixed, weight_grad)


def solution(mesh):
    placed = (
        P("fsdp", "bal", None),
        P("fsdp", "bal", None),
        P("fsdp", "bal", None),
        P("fsdp", "bal", None),
        P("fsdp", None),
        P("fsdp", None),
    )
    return jax.shard_map(
        local,
        mesh=mesh,
        in_specs=placed,
        out_specs=(P("fsdp", "bal", None), P("fsdp", None)),
        check_vma=False,
    )
```

profile of v0, /device:TPU:1, one launch (start us, length us, event | category | flops | bytes accessed | tf_op | source)
XLA Modules:
  0.0 569.3 jit_solution(15102135069156524161)
XLA Ops:
  7.2 1.0 dynamic-slice_reduce_fusion
  8.3 0.6 gather_fusion
  9.0 0.6 copy.20
  9.6 17.6 %all-to-all-start = ((bf16[32,1,8]{2,1,0:T(2,128)(2,1)}), bf16[32,1,8]{2,1,0:T(2,128)(2,1)S(1)}, u32[]{:S(2)}, u32[]{:S(2)}) async-start(bf16[32,1,8]{2,1,0:T(2,128)(2,1)} %copy.20), calls=%async_computation | async-start | bytes 32768 | tf_op jit(solution)/shard_map/all_to_all | solution.py:51
  27.2 1.6 gather_fusion.3
  28.9 1.6 gather_fusion.2
  30.5 0.6 gather_fusion.1
  31.1 1.0 select_bitcast_fusion.2
  32.1 2.1 all-to-all-done
  34.2 16.7 %all_to_all.20 = bf16[32,1,8,1024]{3,2,1,0:T(8,128)(2,1)S(1)} all-to-all(bf16[32,1,8,1024]{3,2,1,0:T(8,128)(2,1)S(1)} %get-tuple-element.9), channel_id=1, replica_groups=mesh['fsdp'=32,'bal'=32] {'bal'}, dimensions={0} | all-to-all | bytes 1048576 | tf_op jit(solution)/shard_map/all_to_all | solution.py:50
  50.9 15.2 %all_to_all.21 = bf16[32,1,8,1024]{3,2,1,0:T(8,128)(2,1)S(1)} all-to-all(bf16[32,1,8,1024]{3,2,1,0:T(8,128)(2,1)S(1)} %get-tuple-element.10), channel_id=1, replica_groups=mesh['fsdp'=32,'bal'=32] {'bal'}, dimensions={0} | all-to-all | bytes 1048576 | tf_op jit(solution)/shard_map/all_to_all | solution.py:48
  66.1 4.0 all-to-all-start.3
  70.6 11.2 %all-to-all-done.3 = bf16[32,1,8,1024]{3,2,1,0:T(8,128)(2,1)S(1)} async-done(((bf16[32,1,8,1024]{3,2,1,0:T(8,128)(2,1)}), bf16[32,1,8,1024]{3,2,1,0:T(8,128)(2,1)S(1)}, u32[]{:S(2)}, u32[]{:S(2)}) %all-to-all-start.3) | async-done | bytes 524320 | tf_op jit(solution)/shard_map/all_to_all | solution.py:49
  81.9 2.2 fusion.30
  84.1 2.0 fusion.3
  86.0 1.0 copy.25
  87.0 0.5 broadcast.78
  87.5 4.2 reduce.8
  91.7 0.3 reshape.202
  92.1 15.2 %all_to_all.22 = bf16[32,2,4096]{2,1,0:T(2,128)(2,1)S(1)} all-to-all(bf16[32,2,4096]{2,1,0:T(2,128)(2,1)S(1)} %reshape.202), channel_id=1, replica_groups=mesh['fsdp'=32,'bal'=32] {'bal'}, dimensions={0} | all-to-all | bytes 1048576 | tf_op jit(solution)/shard_map/all_to_all | solution.py:30
  107.3 0.5 reshape.203
  107.8 0.2 copy.57
  108.0 0.6 gather_fusion.4
  108.6 2.8 convolution_bitcast_fusion
  111.4 5.3 copy.28
  116.8 0.7 all-gather.2.cloned.1.call-update
  117.6 115.2 %reduce-scatter.4.cloned.1.call-done = f32[32,1024]{1,0:T(8,128)} async-done(((f32[1024,1024]{1,0:T(8,128)}), f32[32,1024]{1,0:T(8,128)}) %reduce-scatter.4.cloned.1.call-update) | async-done | bytes 131088
  232.8 1.9 copy.29
  234.7 136.1 %all-gather.2.cloned.1.call-done = bf16[1024,1024]{1,0:T(8,128)(2,1)} async-done(((bf16[32,1024]{1,0:T(8,128)(2,1)}), bf16[1024,1024]{1,0:T(8,128)(2,1)}) %all-gather.2.cloned.1.call-update) | async-done | bytes 2097168 | tf_op jit(solution)/shard_map/all_gather | solution.py:58
  370.8 3.2 fusion.4
  374.0 186.9 %all-reduce.2.cloned.1.call-done = f32[32,1024]{0,1:T(8,128)} async-done(((f32[32,1024]{0,1:T(8,128)}), f32[32,1024]{0,1:T(8,128)}) %all-reduce.2.cloned.1.call-update) | async-done | bytes 131088 | tf_op jit(solution)/shard_map/psum | solution.py:73
  560.9 1.9 copy.26
  (19 shorter events, 0.8 us)
Async XLA Ops:
  7.2 101.4 %copy-start = (bf16[32,8,1024]{2,1,0:T(8,128)(2,1)S(1)}, bf16[32,8,1024]{2,1,0:T(8,128)(2,1)}, u32[]{:S(2)}) copy-start(bf16[32,8,1024]{2,1,0:T(8,128)(2,1)} %param.11) | copy-start | bytes 1572868
  7.2 23.3 %copy-start.1 = (bf16[32,8,1024]{2,1,0:T(8,128)(2,1)S(1)}, bf16[32,8,1024]{2,1,0:T(8,128)(2,1)}, u32[]{:S(2)}) copy-start(bf16[32,8,1024]{2,1,0:T(8,128)(2,1)} %param.10) | copy-start | bytes 1572868
  9.6 24.6 %all-to-all-start = ((bf16[32,1,8]{2,1,0:T(2,128)(2,1)}), bf16[32,1,8]{2,1,0:T(2,128)(2,1)S(1)}, u32[]{:S(2)}, u32[]{:S(2)}) async-start(bf16[32,1,8]{2,1,0:T(2,128)(2,1)} %copy.20), calls=%async_computation | async-start | bytes 32768 | tf_op jit(solution)/shard_map/all_to_all | solution.py:51
  66.1 15.7 %all-to-all-start.3 = ((bf16[32,1,8,1024]{3,2,1,0:T(8,128)(2,1)}), bf16[32,1,8,1024]{3,2,1,0:T(8,128)(2,1)S(1)}, u32[]{:S(2)}, u32[]{:S(2)}) async-start(bf16[32,1,8,1024]{3,2,1,0:T(8,128)(2,1)} %get-tuple-element.11), calls=%async_computation.3 | async-start | bytes 1048576 | tf_op jit(solution)/shard_map/all_to_all | solution.py:49
  70.1 162.6 %reduce-scatter.4.cloned.1.call-start = ((), (), s32[]{:S(2)}) async-start(), calls=%async_computation.8 | async-start | bytes 4325376
  116.8 254.0 %all-gather.2.cloned.1.call-start = ((), (), s32[]{:S(2)}) async-start(), calls=%async_computation.6 | async-start | bytes 2162688 | tf_op jit(solution)/shard_map/all_gather | solution.py:58
  117.5 443.3 %all-reduce.2.cloned.1.call-start = ((), (), s32[]{:S(2)}) async-start(), calls=%async_computation.7 | async-start | bytes 1048576 | tf_op jit(solution)/shard_map/psum | solution.py:73
Sparse Core Ops, SparseCore 0:
  116.9 115.8 reduce-scatter.3
  235.4 135.3 all-gather.1
  374.0 186.8 all-reduce.1
where the time goes:
time: 570 us; the launch traced here: 569 us
  waiting for transfers between devices  452 us (79%)
  blocking collectives  47.2 us (8%)
  starting transfers between devices  21.7 us (4%)
  local copies, waits for them, and re-layouts  18.7 us (3%)
  between operations  13.9 us (2%)
  matrix products  10.1 us (2%)
    psum x1, waiting for transfers between devices, local(): weight_grad = lax.psum(group_rows, 'bal')  187 us
    all_gather x1, waiting for transfers between devices, local(): lax.all_gather(out_weight, 'fsdp', axis=0, tiled=True)  136 us
    unnamed x4, waiting for transfers between devices  116 us
    all_to_all x1, starting transfers between devices, local(): lax.all_to_all(mask_send, 'bal', split_axis=0, concat_axis=2, tiled=True)  17.6 us
    all_to_all x1, blocking collectives, local(): lax.all_to_all(value_send, 'bal', split_axis=0, concat_axis=2, tiled=True)  16.7 us
    all_to_all x1, blocking collectives, attend_items(): lax.all_to_all(attended, 'bal', split_axis=2, concat_axis=0, tiled=True)  15.2 us
    all_to_all x1, blocking collectives, local(): lax.all_to_all(query_send, 'bal', split_axis=0, concat_axis=2, tiled=True)  15.2 us
  transfers between devices with their start and end apart: 5, of which 5 were waited for; matrix products, arithmetic and copies ran while one was open for 2% of the time, Pallas kernels for 0%

commit v1 on v0

v1 whole, which is shorter than its diff:
```python
import functools

import jax
import jax.numpy as jnp
from jax import lax
from jax.experimental import pallas as pl
from jax.experimental.pallas import tpu as pltpu
from jax.sharding import PartitionSpec as P

HEAD_DIM = 128
GROUPS = 4
MESH = pl.DeviceIdType.MESH
BF16 = jnp.bfloat16
F32 = jnp.float32


def remote(src, dst, send_sem, recv_sem, target):
    return pltpu.make_async_remote_copy(
        src_ref=src,
        dst_ref=dst,
        send_sem=send_sem,
        recv_sem=recv_sem,
        device_id=target,
        device_id_type=MESH,
    )


def await_bytes(ref, sem):
    pltpu.make_async_copy(ref, ref, sem).wait()


def flat_rows(block):
    cells, genes, cols = block.shape
    return block.astype(F32).reshape(cells * genes, cols).astype(BF16)


def kernel(
    nz, nb, q, k, v, cot, w, counts, mixed_out, grad_out,
    qkv, att_s, att_h, cot_v, cot_p, wbuf, counts_v, mixed_v, att_2d,
    mine, pair_s, pair_r, rs_s, rs_r, z_32, z_s, z_r, row_s, row_r, grad_v,
    s_qkv, r_qkv, s_att, r_att, s_ring, r_right, r_left, s_sib, r_sib,
    s_pair, r_pair, s_rs, r_rs, s_z, r_z, s_row, r_row, local_sem, out_sem,
):
    my_z, me = lax.axis_index("fsdp"), lax.axis_index("bal")
    core, chip = lax.rem(me, 2), me // 2
    sibling = {"bal": chip * 2 + (1 - core)}
    chips = nb // 2
    width = qkv.shape[-1]
    group_cols = width // GROUPS
    heads_per = group_cols // HEAD_DIM
    half = w.shape[0] // 2
    rows = nb * 8
    features = nz * nb

    def cols_of(g):
        return pl.ds(pl.multiple_of(g * group_cols, group_cols), group_cols)

    barrier = pltpu.get_barrier_semaphore()

    @pl.loop(1, nb)
    def _(i):
        pl.semaphore_signal(barrier, 1, device_id={"bal": lax.rem(me + i, nb)}, device_id_type=MESH)

    @pl.loop(1, nz)
    def _(i):
        pl.semaphore_signal(barrier, 1, device_id={"fsdp": lax.rem(my_z + i, nz)}, device_id_type=MESH)

    load_cot = pltpu.make_async_copy(cot, cot_v, local_sem.at[0])
    load_counts = pltpu.make_async_copy(counts, counts_v, local_sem.at[1])
    load_w0 = pltpu.make_async_copy(w.at[pl.ds(0, half)], wbuf.at[my_z, 0], local_sem.at[2])
    load_w1 = pltpu.make_async_copy(w.at[pl.ds(half, half)], wbuf.at[my_z, 1], local_sem.at[3])
    for load in (load_cot, load_counts, load_w0, load_w1):
        load.start()

    pl.semaphore_wait(barrier, nb + nz - 2)
    load_w0.wait()
    load_w1.wait()

    right, left = {"fsdp": lax.rem(my_z + 1, nz)}, {"fsdp": lax.rem(my_z + nz - 1, nz)}
    right_hops, left_hops = nz // 2, nz // 2 - 1

    def ring_right(step):
        block = wbuf.at[lax.rem(my_z + nz - step, nz), core]
        remote(block, block, s_ring, r_right.at[step], right).start()

    def ring_left(step):
        block = wbuf.at[lax.rem(my_z + step, nz), core]
        remote(block, block, s_ring, r_left.at[step], left).start()

    def ring_step(step):
        block = wbuf.at[lax.rem(my_z + nz - step, nz), core]
        await_bytes(block, r_right.at[step - 1])

        @pl.when(step < right_hops)
        def _():
            ring_right(step)

        remote(block, block, s_sib, r_sib, sibling).start()

        @pl.when(step <= left_hops)
        def _():
            other = wbuf.at[lax.rem(my_z + step, nz), core]
            await_bytes(other, r_left.at[step - 1])

            @pl.when(step < left_hops)
            def _():
                ring_left(step)

            remote(other, other, s_sib, r_sib, sibling).start()

    ring_right(0)
    ring_left(0)

    for g in range(GROUPS):
        cols = pl.ds(g * group_cols, group_cols)
        for a, ref in enumerate((q, k, v)):
            pltpu.make_async_copy(ref.at[me, :, cols], qkv.at[a, me, :, cols], r_qkv.at[g]).start()

        @pl.loop(1, nb)
        def _(i):
            peer = lax.rem(me + i, nb)
            for a, ref in enumerate((q, k, v)):
                remote(
                    ref.at[peer, :, cols], qkv.at[a, me, :, cols], s_qkv, r_qkv.at[g], {"bal": peer}
                ).start()

    load_cot.wait()
    load_counts.wait()
    cot_2d = flat_rows(cot_v[...])
    step_rows = min(256, features)

    @pl.loop(0, features // step_rows)
    def _(n):
        shape = (step_rows, features)
        m = lax.broadcasted_iota(jnp.int32, shape, 0) + n * step_rows
        f = lax.broadcasted_iota(jnp.int32, shape, 1)
        source = (m % nz) * nb + ((m // nz) % chips) * 2 + m // (nz * chips)
        chosen = jnp.where(f == source, 1.0, 0.0).astype(BF16)
        out = lax.dot_general(chosen, cot_2d, (((1,), (1,)), ((), ())), preferred_element_type=F32)
        cot_p[pl.ds(pl.multiple_of(n * step_rows, step_rows), step_rows), :] = out.astype(BF16)

    my_counts = counts_v[pl.ds(me, 1), :].astype(F32)
    spread = lax.broadcasted_iota(jnp.int32, (rows, nb), 0) // 8 == lax.broadcasted_iota(
        jnp.int32, (rows, nb), 1
    )
    picked = jnp.where(spread, jnp.broadcast_to(my_counts, (rows, nb)), 0.0)
    row_count = jnp.sum(picked, axis=1, keepdims=True)
    slot = (lax.broadcasted_iota(jnp.int32, (rows, 1), 0) % 8).astype(F32)
    row_live = slot < row_count
    gather = (
        lax.broadcasted_iota(jnp.int32, (nb, rows), 1) // 8 == lax.broadcasted_iota(jnp.int32, (nb, rows), 0)
    )
    col_count = lax.dot_general(
        jnp.broadcast_to(my_counts, (8, nb)).astype(BF16),
        jnp.where(gather, 1.0, 0.0).astype(BF16),
        (((1,), (0,)), ((), ())),
        preferred_element_type=F32,
    )[0:1, :]
    col_slot = (lax.broadcasted_iota(jnp.int32, (1, rows), 1) % 8).astype(F32)
    col_live = col_slot < col_count
    scale = HEAD_DIM ** (-0.5)

    ring_per = -(-right_hops // GROUPS)

    def ring_some(g):
        for j in range(ring_per):
            step = g * ring_per + j + 1

            @pl.when(step <= right_hops)
            def _():
                ring_step(step)

    @pl.loop(0, GROUPS)
    def _(g):
        ring_some(g)
        cols = cols_of(g)
        await_bytes(qkv.at[:, :, :, cols], r_qkv.at[g])
        for h in range(heads_per):
            head = pl.ds(pl.multiple_of(g * group_cols + h * HEAD_DIM, HEAD_DIM), HEAD_DIM)
            qh = flat_rows(qkv[0, :, :, head])
            kh = flat_rows(qkv[1, :, :, head])
            vh = flat_rows(qkv[2, :, :, head])
            scores = lax.dot_general(qh, kh, (((1,), (1,)), ((), ())), preferred_element_type=F32)
            scores = jnp.where(col_live, scores * scale, -1e30)
            peak = jnp.max(scores, axis=1, keepdims=True)
            expo = jnp.exp(scores - peak)
            total = jnp.sum(expo, axis=1, keepdims=True)
            probs = (expo * (1.0 / total)).astype(BF16)
            out = lax.dot_general(probs, vh, (((1,), (0,)), ((), ())), preferred_element_type=F32)
            out = jnp.where(row_live, out, 0.0)
            att_s[:, :, head] = out.reshape(nb, 8, HEAD_DIM).astype(BF16)
        pltpu.make_async_copy(att_s.at[me, :, cols], att_h.at[me, :, cols], r_att.at[g]).start()

        @pl.loop(1, nb)
        def _(i):
            peer = lax.rem(me + i, nb)
            remote(
                att_s.at[peer, :, cols], att_h.at[me, :, cols], s_att, r_att.at[g], {"bal": peer}
            ).start()

    half_rows = features // 2

    @pl.loop(0, GROUPS)
    def _(g):
        cols = cols_of(g)
        await_bytes(att_h.at[:, :, cols], r_att.at[g])
        a2 = flat_rows(att_h[:, :, cols])
        att_2d[:, cols] = a2
        their_rows = pl.ds(pl.multiple_of((1 - core) * half_rows, half_rows), half_rows)
        pair_s[g] = jnp.dot(cot_p[their_rows, :], a2, preferred_element_type=F32).astype(BF16)
        remote(pair_s.at[g], pair_r.at[g], s_pair, r_pair.at[g], sibling).start()
        my_rows = pl.ds(pl.multiple_of(core * half_rows, half_rows), half_rows)
        mine[g] = jnp.dot(cot_p[my_rows, :], a2, preferred_element_type=F32)

    @pl.loop(0, GROUPS)
    def _(g):
        await_bytes(pair_r.at[g], r_pair.at[g])
        both = mine[g] + pair_r[g].astype(F32)
        rs_s[g] = both.reshape(chips, nz, group_cols).astype(BF16)
        pltpu.make_async_copy(rs_s.at[g, chip], rs_r.at[g, chip], r_rs.at[g]).start()

        @pl.loop(1, chips)
        def _(i):
            peer = lax.rem(chip + i, chips)
            remote(
                rs_s.at[g, peer], rs_r.at[g, chip], s_rs, r_rs.at[g], {"bal": peer * 2 + core}
            ).start()

    await_bytes(wbuf.at[pl.ds(0, nz - 1), 0], r_sib)
    blocks = 8 if nz % 8 == 0 else nz
    out_cols = blocks * 2 * half

    @pl.loop(0, nz // blocks)
    def _(n):
        wn = wbuf[pl.ds(n * blocks, blocks)].reshape(out_cols, width)
        out = lax.dot_general(att_2d[...], wn, (((1,), (1,)), ((), ())), preferred_element_type=F32)
        out_at = pl.ds(pl.multiple_of(n * out_cols, out_cols), out_cols)
        mixed_v[:, :, out_at] = out.reshape(nb, 8, out_cols).astype(BF16)

    store_mixed = pltpu.make_async_copy(mixed_v, mixed_out, out_sem.at[0])
    store_mixed.start()

    for g in range(GROUPS):
        await_bytes(rs_r.at[g], r_rs.at[g])
        plane = jnp.sum(rs_r[g].astype(F32), axis=0)
        for t in range(group_cols // 128):
            z_32[pl.ds(g * (group_cols // 128) + t, nz, stride=8), :] = plane[:, t * 128 : (t + 1) * 128]
    z_s[...] = z_32[...].reshape(nz, 8, 128).astype(BF16)
    pltpu.make_async_copy(z_s.at[my_z], z_r.at[my_z], r_z).start()

    @pl.loop(1, nz)
    def _(i):
        peer = lax.rem(my_z + i, nz)
        remote(z_s.at[peer], z_r.at[my_z], s_z, r_z, {"fsdp": peer}).start()

    await_bytes(z_r, r_z)
    row_s[...] = jnp.sum(z_r[...].astype(F32), axis=0)
    pltpu.make_async_copy(row_s, row_r.at[me], r_row).start()

    @pl.loop(1, nb)
    def _(i):
        peer = lax.rem(me + i, nb)
        remote(row_s, row_r.at[me], s_row, r_row, {"bal": peer}).start()

    await_bytes(row_r, r_row)
    for t in range(8):
        grad_v[:, t * 128 : (t + 1) * 128] = row_r[:, t, :]
    store_grad = pltpu.make_async_copy(grad_v, grad_out, out_sem.at[1])
    store_grad.start()

    await_bytes(qkv.at[:, pl.ds(0, nb - 1)], s_qkv)
    await_bytes(att_s.at[pl.ds(0, nb - 1)], s_att)
    await_bytes(wbuf.at[pl.ds(0, nz - 1), 0], s_ring)
    await_bytes(wbuf.at[pl.ds(0, nz - 1), 0], s_sib)
    await_bytes(pair_s, s_pair)
    await_bytes(rs_s.at[:, pl.ds(0, chips - 1)], s_rs)
    await_bytes(z_s.at[pl.ds(0, nz - 1)], s_z)
    await_bytes(row_r.at[pl.ds(0, nb - 1)], s_row)
    store_mixed.wait()
    store_grad.wait()


def local(nz, nb, query_rows, key_rows, value_rows, cotangent, out_weight, token_counts):
    cells, genes, width = query_rows.shape
    shard = out_weight.shape[0]
    features = nz * shard
    rows = cells * genes
    group_cols = width // GROUPS
    chips = nb // 2
    vmem = pltpu.VMEM
    dma = pltpu.SemaphoreType.DMA
    scratch = [
        vmem((3, nb, genes, width), BF16),
        vmem((nb, genes, width), BF16),
        vmem((nb, genes, width), BF16),
        vmem((nb, genes, features), BF16),
        vmem((features, rows), BF16),
        vmem((nz, 2, shard // 2, width), BF16),
        vmem(token_counts.shape, jnp.int32),
        vmem((nb, genes, features), BF16),
        vmem((rows, width), BF16),
        vmem((GROUPS, features // 2, group_cols), F32),
        vmem((GROUPS, features // 2, group_cols), BF16),
        vmem((GROUPS, features // 2, group_cols), BF16),
        vmem((GROUPS, chips, nz, group_cols), BF16),
        vmem((GROUPS, chips, nz, group_cols), BF16),
        vmem((nz * 8, 128), F32),
        vmem((nz, 8, 128), BF16),
        vmem((nz, 8, 128), BF16),
        vmem((8, 128), F32),
        vmem((nb, 8, 128), F32),
        vmem((shard, width), F32),
        dma, dma((GROUPS,)),
        dma, dma((GROUPS,)),
        dma, dma((nz // 2,)), dma((nz // 2,)),
        dma, dma,
        dma, dma((GROUPS,)),
        dma, dma((GROUPS,)),
        dma, dma,
        dma, dma,
        dma((4,)),
        dma((2,)),
    ]
    any_spec = pl.BlockSpec(memory_space=pl.ANY)
    return pl.pallas_call(
        functools.partial(kernel, nz, nb),
        out_shape=(
            jax.ShapeDtypeStruct((cells, genes, features), BF16),
            jax.ShapeDtypeStruct((shard, width), F32),
        ),
        in_specs=[any_spec] * 6,
        out_specs=(any_spec, any_spec),
        scratch_shapes=scratch,
        compiler_params=pltpu.CompilerParams(
            collective_id=0, has_side_effects=True, vmem_limit_bytes=48 * 1024 * 1024
        ),
        name="attend_project",
    )(query_rows, key_rows, value_rows, cotangent, out_weight, token_counts)


def solution(mesh):
    nz, nb = mesh.shape["fsdp"], mesh.shape["bal"]
    placed = (
        P("fsdp", "bal", None),
        P("fsdp", "bal", None),
        P("fsdp", "bal", None),
        P("fsdp", "bal", None),
        P("fsdp", None),
        P("fsdp", None),
    )
    return jax.shard_map(
        functools.partial(local, nz, nb),
        mesh=mesh,
        in_specs=placed,
        out_specs=(P("fsdp", "bal", None), P("fsdp", None)),
        check_vma=False,
    )
```

time: 570 us -> 133 us (0.23)
  waiting for transfers between devices: 452 us -> 0 us
  Pallas kernels: 0 us -> 125 us
  blocking collectives: 47.2 us -> 0 us
  starting transfers between devices: 21.7 us -> 0 us
  between operations: 13.9 us -> 0.65 us
  local copies, waits for them, and re-layouts: 18.7 us -> 7.16 us
  matrix products: 10.1 us -> 0 us
    psum x1 -> x0, waiting for transfers between devices: 187 us -> none  [local(): weight_grad = lax.psum(group_rows, 'bal')]
    all_gather x1 -> x0, waiting for transfers between devices: 136 us -> none  [local(): lax.all_gather(out_weight, 'fsdp', axis=0, tiled=True)]
    pallas_call x0 -> x1, Pallas kernels: none -> 125 us  [local(): pl.pallas_call(functools.partial(kernel, nz, nb), out_shape=(jax.ShapeDty...]
    unnamed x4 -> x0, waiting for transfers between devices: 116 us -> none
    all_to_all x3 -> x0, blocking collectives: 47.2 us -> none  [the longest x1 16.7 us: local(): lax.all_to_all(value_send, 'bal', split_axis=0, concat_axis=2, tiled=True)]
    all_to_all x2 -> x0, starting transfers between devices: 21.6 us -> none  [the longest x1 17.6 us: local(): lax.all_to_all(mask_send, 'bal', split_axis=0, concat_axis=2, tiled=True)]
    all_to_all x2 -> x0, waiting for transfers between devices: 13.4 us -> none  [the longest x1 11.2 us: local(): lax.all_to_all(key_send, 'bal', split_axis=0, concat_axis=2, tiled=True)]
    dot_general x3 -> x0, matrix products: 7.92 us -> none  [the longest x1 3.16 us: local(): lax.dot_general(attended_flat, lax.all_gather(out_weight, 'fsdp', axis=0,...]
  transfers between devices with their start and end apart: 5 -> 0, of which waited for: 5 -> 0; matrix products, arithmetic and copies ran while one was open for 2% -> 0% of each run, Pallas kernels for 0% -> 0%
where the time goes in v1:
time: 133 us
  Pallas kernels  125 us (94%)
  local copies, waits for them, and re-layouts  7.16 us (5%)
    pallas_call x1, Pallas kernels, local(): pl.pallas_call(functools.partial(kernel, nz, nb), out_shape=(jax.ShapeDty...  125 us
    unnamed x14, local copies, waits for them, and re-layouts  7.16 us

profile of v1, /device:TPU:1, one launch (start us, length us, event | category | flops | bytes accessed | tf_op | source)
XLA Modules:
  0.0 132.6 jit_solution(4018080212462546523)
XLA Ops:
  0.6 0.0 copy-start
  0.6 1.0 copy-done
  1.7 0.0 copy-start.1
  1.7 1.0 copy-done.1
  2.7 0.0 copy-start.2
  2.7 1.0 copy-done.2
  3.8 0.0 copy-start.3
  3.8 1.0 copy-done.3
  4.8 0.0 copy-start.4
  4.8 0.8 copy-done.4
  5.6 0.0 copy-start.5
  5.6 0.7 copy-done.5
  6.4 124.7 %attend_project.1 = (bf16[32,8,1024]{2,1,0:T(8,128)(2,1)S(1)}, f32[32,1024]{1,0:T(8,128)S(1)}) custom-call(bf16[32,8,1024]{2,1,0:T(8,128)(2,1)S(1)} %copy-done, bf16[32,8,1024]{2,1,0:T(8,128)(2,1)S(1)} %copy-done.1, bf16[32,8,1024]{2,1,0:T(8,128)(2,1)S(1)} %copy-done.2, bf16[32,8,1024]{2,1,0:T(8,128)(2,1)S(1)} %copy-done.3, bf16[32,1024]{1,0:T(8,128)(2,1)S(1)} %copy-done.4, ...), custom_call_target="tpu_custom_call" | custom-call | tf_op jit(solution)/shard_map/attend_project/pallas_call | solution.py:325
  131.1 0.8 copy.10
  131.9 0.7 copy.11
Async XLA Ops:
  0.6 1.0 copy-start
  1.7 1.0 copy-start.1
  2.7 1.0 copy-start.2
  3.8 1.0 copy-start.3
  4.8 0.8 copy-start.4
  5.6 0.7 copy-start.5

commit v2 on v1

--- a/solution.py
+++ b/solution.py
@@ -34,11 +34,15 @@
     return block.astype(F32).reshape(cells * genes, cols).astype(BF16)
 
 
+def far_first(i, n):
+    return n // 2 + ((i + 1) // 2) * (1 - 2 * (i % 2))
+
+
 def kernel(
     nz, nb, q, k, v, cot, w, counts, mixed_out, grad_out,
-    qkv, att_s, att_h, cot_v, cot_p, wbuf, counts_v, mixed_v, att_2d,
+    stage, qkv, att_s, att_h, cot_v, cot_p, w_v, w_st, wz, wfull, counts_v, mixed_v, att_2d,
     mine, pair_s, pair_r, rs_s, rs_r, z_32, z_s, z_r, row_s, row_r, grad_v,
-    s_qkv, r_qkv, s_att, r_att, s_ring, r_right, r_left, s_sib, r_sib,
+    s_qkv, r_qkv, s_att, r_att, s_wz, r_wz, s_wa, r_wa, s_sib, r_sib,
     s_pair, r_pair, s_rs, r_rs, s_z, r_z, s_row, r_row, local_sem, out_sem,
 ):
     my_z, me = lax.axis_index("fsdp"), lax.axis_index("bal")
@@ -48,7 +52,7 @@
     width = qkv.shape[-1]
     group_cols = width // GROUPS
     heads_per = group_cols // HEAD_DIM
-    half = w.shape[0] // 2
+    half_width = width // 2
     rows = nb * 8
     features = nz * nb
 
@@ -65,64 +69,45 @@
     def _(i):
         pl.semaphore_signal(barrier, 1, device_id={"fsdp": lax.rem(my_z + i, nz)}, device_id_type=MESH)
 
-    load_cot = pltpu.make_async_copy(cot, cot_v, local_sem.at[0])
-    load_counts = pltpu.make_async_copy(counts, counts_v, local_sem.at[1])
-    load_w0 = pltpu.make_async_copy(w.at[pl.ds(0, half)], wbuf.at[my_z, 0], local_sem.at[2])
-    load_w1 = pltpu.make_async_copy(w.at[pl.ds(half, half)], wbuf.at[my_z, 1], local_sem.at[3])
-    for load in (load_cot, load_counts, load_w0, load_w1):
+    loads = [
+        pltpu.make_async_copy(ref, stage.at[:, a], local_sem.at[a]) for a, ref in enumerate((q, k, v))
+    ]
+    load_w = pltpu.make_async_copy(w, w_v, local_sem.at[3])
+    load_cot = pltpu.make_async_copy(cot, cot_v, local_sem.at[4])
+    load_counts = pltpu.make_async_copy(counts, counts_v, local_sem.at[5])
+    for load in (*loads, load_w, load_cot, load_counts):
         load.start()
 
+    load_w.wait()
+    shard = w_v[...].astype(F32)
+    for a in range(w_v.shape[0] // 8):
+        for t in range(width // 128):
+            w_st[a, t] = shard[a * 8 : a * 8 + 8, t * 128 : t * 128 + 128].astype(BF16)
+    tile_row, tile_col = chip // 4, chip % 4 + 4 * core
+    for load in loads:
+        load.wait()
     pl.semaphore_wait(barrier, nb + nz - 2)
-    load_w0.wait()
-    load_w1.wait()
-
-    right, left = {"fsdp": lax.rem(my_z + 1, nz)}, {"fsdp": lax.rem(my_z + nz - 1, nz)}
-    right_hops, left_hops = nz // 2, nz // 2 - 1
-
-    def ring_right(step):
-        block = wbuf.at[lax.rem(my_z + nz - step, nz), core]
-        remote(block, block, s_ring, r_right.at[step], right).start()
-
-    def ring_left(step):
-        block = wbuf.at[lax.rem(my_z + step, nz), core]
-        remote(block, block, s_ring, r_left.at[step], left).start()
-
-    def ring_step(step):
-        block = wbuf.at[lax.rem(my_z + nz - step, nz), core]
-        await_bytes(block, r_right.at[step - 1])
-
-        @pl.when(step < right_hops)
-        def _():
-            ring_right(step)
-
-        remote(block, block, s_sib, r_sib, sibling).start()
-
-        @pl.when(step <= left_hops)
-        def _():
-            other = wbuf.at[lax.rem(my_z + step, nz), core]
-            await_bytes(other, r_left.at[step - 1])
-
-            @pl.when(step < left_hops)
-            def _():
-                ring_left(step)
-
-            remote(other, other, s_sib, r_sib, sibling).start()
-
-    ring_right(0)
-    ring_left(0)
-
-    for g in range(GROUPS):
-        cols = pl.ds(g * group_cols, group_cols)
-        for a, ref in enumerate((q, k, v)):
-            pltpu.make_async_copy(ref.at[me, :, cols], qkv.at[a, me, :, cols], r_qkv.at[g]).start()
+
+    def send_qkv(g):
+        cols = cols_of(g)
+        pltpu.make_async_copy(stage.at[me, :, :, cols], qkv.at[me, :, :, cols], r_qkv.at[g]).start()
 
         @pl.loop(1, nb)
         def _(i):
             peer = lax.rem(me + i, nb)
-            for a, ref in enumerate((q, k, v)):
-                remote(
-                    ref.at[peer, :, cols], qkv.at[a, me, :, cols], s_qkv, r_qkv.at[g], {"bal": peer}
-                ).start()
+            remote(
+                stage.at[peer, :, :, cols], qkv.at[me, :, :, cols], s_qkv, r_qkv.at[g], {"bal": peer}
+            ).start()
+
+    send_qkv(0)
+    pltpu.make_async_copy(w_st.at[tile_row, tile_col], wz.at[my_z], r_wz).start()
+
+    @pl.loop(0, nz - 1)
+    def _(i):
+        peer = lax.rem(my_z + far_first(i, nz), nz)
+        remote(w_st.at[tile_row, tile_col], wz.at[my_z], s_wz, r_wz, {"fsdp": peer}).start()
+
+    send_qkv(1)
 
     load_cot.wait()
     load_counts.wait()
@@ -159,27 +144,16 @@
     col_slot = (lax.broadcasted_iota(jnp.int32, (1, rows), 1) % 8).astype(F32)
     col_live = col_slot < col_count
     scale = HEAD_DIM ** (-0.5)
-
-    ring_per = -(-right_hops // GROUPS)
-
-    def ring_some(g):
-        for j in range(ring_per):
-            step = g * ring_per + j + 1
-
-            @pl.when(step <= right_hops)
-            def _():
-                ring_step(step)
-
-    @pl.loop(0, GROUPS)
-    def _(g):
-        ring_some(g)
+    half_rows = features // 2
+
+    def attend(g):
         cols = cols_of(g)
         await_bytes(qkv.at[:, :, :, cols], r_qkv.at[g])
         for h in range(heads_per):
             head = pl.ds(pl.multiple_of(g * group_cols + h * HEAD_DIM, HEAD_DIM), HEAD_DIM)
-            qh = flat_rows(qkv[0, :, :, head])
-            kh = flat_rows(qkv[1, :, :, head])
-            vh = flat_rows(qkv[2, :, :, head])
+            qh = flat_rows(qkv[:, 0, :, head])
+            kh = flat_rows(qkv[:, 1, :, head])
+            vh = flat_rows(qkv[:, 2, :, head])
             scores = lax.dot_general(qh, kh, (((1,), (1,)), ((), ())), preferred_element_type=F32)
             scores = jnp.where(col_live, scores * scale, -1e30)
             peak = jnp.max(scores, axis=1, keepdims=True)
@@ -198,10 +172,7 @@
                 att_s.at[peer, :, cols], att_h.at[me, :, cols], s_att, r_att.at[g], {"bal": peer}
             ).start()
 
-    half_rows = features // 2
-
-    @pl.loop(0, GROUPS)
-    def _(g):
+    def share(g):
         cols = cols_of(g)
         await_bytes(att_h.at[:, :, cols], r_att.at[g])
         a2 = flat_rows(att_h[:, :, cols])
@@ -212,8 +183,7 @@
         my_rows = pl.ds(pl.multiple_of(core * half_rows, half_rows), half_rows)
         mine[g] = jnp.dot(cot_p[my_rows, :], a2, preferred_element_type=F32)
 
-    @pl.loop(0, GROUPS)
-    def _(g):
+    def scatter(g):
         await_bytes(pair_r.at[g], r_pair.at[g])
         both = mine[g] + pair_r[g].astype(F32)
         rs_s[g] = both.reshape(chips, nz, group_cols).astype(BF16)
@@ -226,19 +196,32 @@
                 rs_s.at[g, peer], rs_r.at[g, chip], s_rs, r_rs.at[g], {"bal": peer * 2 + core}
             ).start()
 
-    await_bytes(wbuf.at[pl.ds(0, nz - 1), 0], r_sib)
-    blocks = 8 if nz % 8 == 0 else nz
-    out_cols = blocks * 2 * half
-
-    @pl.loop(0, nz // blocks)
-    def _(n):
-        wn = wbuf[pl.ds(n * blocks, blocks)].reshape(out_cols, width)
-        out = lax.dot_general(att_2d[...], wn, (((1,), (1,)), ((), ())), preferred_element_type=F32)
-        out_at = pl.ds(pl.multiple_of(n * out_cols, out_cols), out_cols)
-        mixed_v[:, :, out_at] = out.reshape(nb, 8, out_cols).astype(BF16)
-
-    store_mixed = pltpu.make_async_copy(mixed_v, mixed_out, out_sem.at[0])
-    store_mixed.start()
+    @pl.loop(0, GROUPS + 2)
+    def _(t):
+        @pl.when(t < GROUPS)
+        def _():
+            attend(t)
+
+        @pl.when(t + 2 < GROUPS)
+        def _():
+            send_qkv(t + 2)
+
+        @pl.when(t >= 2)
+        def _():
+            scatter(t - 2)
+
+        @pl.when(jnp.logical_and(t >= 1, t < GROUPS + 1))
+        def _():
+            share(t - 1)
+
+    await_bytes(wz, r_wz)
+    tile = wfull.at[:, tile_row, :, pl.ds(pl.multiple_of(tile_col * 128, 128), 128)]
+    pltpu.make_async_copy(wz, tile, r_wa).start()
+
+    @pl.loop(1, chips)
+    def _(i):
+        peer = lax.rem(chip + i, chips)
+        remote(wz, tile, s_wa, r_wa, {"bal": peer * 2 + core}).start()
 
     for g in range(GROUPS):
         await_bytes(rs_r.at[g], r_rs.at[g])
@@ -248,10 +231,14 @@
     z_s[...] = z_32[...].reshape(nz, 8, 128).astype(BF16)
     pltpu.make_async_copy(z_s.at[my_z], z_r.at[my_z], r_z).start()
 
-    @pl.loop(1, nz)
-    def _(i):
-        peer = lax.rem(my_z + i, nz)
+    @pl.loop(0, nz - 1)
+    def _(i):
+        peer = lax.rem(my_z + far_first(i, nz), nz)
         remote(z_s.at[peer], z_r.at[my_z], s_z, r_z, {"fsdp": peer}).start()
+
+    my_half = wfull.at[:, :, :, pl.ds(pl.multiple_of(core * half_width, half_width), half_width)]
+    await_bytes(my_half, r_wa)
+    remote(my_half, my_half, s_sib, r_sib, sibling).start()
 
     await_bytes(z_r, r_z)
     row_s[...] = jnp.sum(z_r[...].astype(F32), axis=0)
@@ -261,6 +248,20 @@
     def _(i):
         peer = lax.rem(me + i, nb)
         remote(row_s, row_r.at[me], s_row, r_row, {"bal": peer}).start()
+
+    await_bytes(my_half, r_sib)
+    blocks = 8 if nz % 8 == 0 else nz
+    out_cols = blocks * nb
+
+    @pl.loop(0, nz // blocks)
+    def _(n):
+        wn = wfull[pl.ds(n * blocks, blocks)].astype(F32).reshape(out_cols, width).astype(BF16)
+        out = lax.dot_general(att_2d[...], wn, (((1,), (1,)), ((), ())), preferred_element_type=F32)
+        out_at = pl.ds(pl.multiple_of(n * out_cols, out_cols), out_cols)
+        mixed_v[:, :, out_at] = out.reshape(nb, 8, out_cols).astype(BF16)
+
+    store_mixed = pltpu.make_async_copy(mixed_v, mixed_out, out_sem.at[0])
+    store_mixed.start()
 
     await_bytes(row_r, r_row)
     for t in range(8):
@@ -268,10 +269,11 @@
     store_grad = pltpu.make_async_copy(grad_v, grad_out, out_sem.at[1])
     store_grad.start()
 
-    await_bytes(qkv.at[:, pl.ds(0, nb - 1)], s_qkv)
+    await_bytes(qkv.at[pl.ds(0, nb - 1)], s_qkv)
     await_bytes(att_s.at[pl.ds(0, nb - 1)], s_att)
-    await_bytes(wbuf.at[pl.ds(0, nz - 1), 0], s_ring)
-    await_bytes(wbuf.at[pl.ds(0, nz - 1), 0], s_sib)
+    await_bytes(wz.at[pl.ds(0, nz - 1)], s_wz)
+    await_bytes(rs_r.at[:, pl.ds(0, chips - 1)], s_wa)
+    await_bytes(my_half, s_sib)
     await_bytes(pair_s, s_pair)
     await_bytes(rs_s.at[:, pl.ds(0, chips - 1)], s_rs)
     await_bytes(z_s.at[pl.ds(0, nz - 1)], s_z)
@@ -290,12 +292,16 @@
     vmem = pltpu.VMEM
     dma = pltpu.SemaphoreType.DMA
     scratch = [
-        vmem((3, nb, genes, width), BF16),
+        vmem((nb, 3, genes, width), BF16),
+        vmem((nb, 3, genes, width), BF16),
         vmem((nb, genes, width), BF16),
         vmem((nb, genes, width), BF16),
         vmem((nb, genes, features), BF16),
         vmem((features, rows), BF16),
-        vmem((nz, 2, shard // 2, width), BF16),
+        vmem((shard, width), BF16),
+        vmem((shard // 8, width // 128, 8, 128), BF16),
+        vmem((nz, 8, 128), BF16),
+        vmem((nz, shard // 8, 8, width), BF16),
         vmem(token_counts.shape, jnp.int32),
         vmem((nb, genes, features), BF16),
         vmem((rows, width), BF16),
@@ -312,13 +318,14 @@
         vmem((shard, width), F32),
         dma, dma((GROUPS,)),
         dma, dma((GROUPS,)),
-        dma, dma((nz // 2,)), dma((nz // 2,)),
+        dma, dma,
+        dma, dma,
         dma, dma,
         dma, dma((GROUPS,)),
         dma, dma((GROUPS,)),
         dma, dma,
         dma, dma,
-        dma((4,)),
+        dma((6,)),
         dma((2,)),
     ]
     any_spec = pl.BlockSpec(memory_space=pl.ANY)
@@ -335,7 +342,7 @@
             collective_id=0, has_side_effects=True, vmem_limit_bytes=48 * 1024 * 1024
         ),
         name="attend_project",
-    )(query_rows, key_rows, value_rows, cotangent, out_weight, token_counts)
+    )(*[pltpu.with_memory_space_constraint(a, pltpu.HBM) for a in (query_rows, key_rows, value_rows, cotangent, out_weight, token_counts)])
 
 
 def solution(mesh):

time: 133 us -> 91.1 us (0.68)
  Pallas kernels: 125 us -> 88.9 us
  local copies, waits for them, and re-layouts: 7.16 us -> 1.45 us
    pallas_call x1, Pallas kernels: 125 us -> 88.9 us  [local(): pl.pallas_call(functools.partial(kernel, nz, nb), out_shape=(jax.ShapeDty...]
    unnamed x14 -> x2, local copies, waits for them, and re-layouts: 7.16 us -> 1.45 us
where the time goes in v2:
time: 91.1 us; the launch traced here: 91 us
  Pallas kernels  88.9 us (98%)
  local copies, waits for them, and re-layouts  1.45 us (2%)
    pallas_call x1, Pallas kernels, local(): pl.pallas_call(functools.partial(kernel, nz, nb), out_shape=(jax.ShapeDty...  88.9 us

profile of v2, /device:TPU:1, one launch (start us, length us, event | category | flops | bytes accessed | tf_op | source)
XLA Modules:
  0.0 91.0 jit_solution(9472283533781528823)
XLA Ops:
  0.6 88.9 %attend_project.1 = (bf16[32,8,1024]{2,1,0:T(8,128)(2,1)S(1)}, f32[32,1024]{1,0:T(8,128)S(1)}) custom-call(bf16[32,8,1024]{2,1,0:T(8,128)(2,1)} %q.1, bf16[32,8,1024]{2,1,0:T(8,128)(2,1)} %k.1, bf16[32,8,1024]{2,1,0:T(8,128)(2,1)} %v.1, bf16[32,8,1024]{2,1,0:T(8,128)(2,1)} %cot.1, bf16[32,1024]{1,0:T(8,128)(2,1)} %w.1, s32[32,32]{1,0:T(8,128)} %counts.1), custom_call_target="tpu_custom_call" | custom-call | tf_op jit(solution)/shard_map/attend_project/pallas_call | solution.py:332
  89.5 0.8 copy.10
  90.3 0.7 copy.11

commit v3 on v2

v3 whole, which is shorter than its diff:
```python
import functools

import jax
import jax.numpy as jnp
from jax import lax
from jax.experimental import pallas as pl
from jax.experimental.pallas import tpu as pltpu
from jax.sharding import PartitionSpec as P

HEAD_DIM = 128
GROUPS = 4
MESH = pl.DeviceIdType.MESH
BF16 = jnp.bfloat16
F32 = jnp.float32


def remote(src, dst, send_sem, recv_sem, target):
    return pltpu.make_async_remote_copy(
        src_ref=src,
        dst_ref=dst,
        send_sem=send_sem,
        recv_sem=recv_sem,
        device_id=target,
        device_id_type=MESH,
    )


def await_bytes(ref, sem):
    pltpu.make_async_copy(ref, ref, sem).wait()


def flat_rows(block):
    cells, genes, cols = block.shape
    return block.astype(F32).reshape(cells * genes, cols).astype(BF16)


def far_first(i, n):
    return n // 2 + ((i + 1) // 2) * (1 - 2 * (i % 2))


def kernel(
    nz, nb, q, k, v, cot, w, counts, mixed_out, grad_out,
    stage, qkv, att_s, att_h, cot_v, cot_p, w_v, w_st, wz, wfull, counts_v, mixed_v, att_2d,
    mine, pair_s, pair_r, kept, two_s, two_r, rs_s, rs_r, z_32, z_s, z_r, row_s, row_r, grad_v,
    s_qkv, r_qkv, s_cot, r_cot, s_att, r_att, s_wf, r_wf, s_wn, r_wn, s_wa, r_wa, s_sib, r_sib,
    s_pair, r_pair, s_two, r_two, s_rs, r_rs, s_z, r_z, s_row, r_row, local_sem, out_sem,
):
    my_z, me = lax.axis_index("fsdp"), lax.axis_index("bal")
    core, chip = lax.rem(me, 2), me // 2
    sibling = {"bal": chip * 2 + (1 - core)}
    chips = nb // 2
    width = qkv.shape[-1]
    group_cols = width // GROUPS
    heads_per = group_cols // HEAD_DIM
    half_width = width // 2
    rows = nb * 8
    features = nz * nb
    high_n, low_n = wz.shape[0], wz.shape[1]
    high, low = my_z // low_n, lax.rem(my_z, low_n)
    x_n = 4
    x_at, y_at = lax.rem(chip, x_n), chip // x_n
    y_n = chips // x_n
    parity, z_half = lax.rem(my_z, 2), my_z // 2
    even_n = nz // 2
    next_z = {"fsdp": my_z + 1 - 2 * parity}

    def near(i):
        return high * low_n + lax.rem(low + i, low_n)

    def far(i):
        return lax.rem(high + i, high_n) * low_n + low

    def cols_of(g):
        return pl.ds(pl.multiple_of(g * group_cols, group_cols), group_cols)

    barrier = pltpu.get_barrier_semaphore()

    @pl.loop(1, nb)
    def _(i):
        pl.semaphore_signal(barrier, 1, device_id={"bal": lax.rem(me + i, nb)}, device_id_type=MESH)

    @pl.loop(1, even_n)
    def _(i):
        peer = lax.rem(z_half + i, even_n) * 2 + parity
        pl.semaphore_signal(barrier, 1, device_id={"fsdp": peer}, device_id_type=MESH)

    pl.semaphore_signal(barrier, 1, device_id=next_z, device_id_type=MESH)
    if low_n == 4:
        mirror = high * low_n + low_n - 1 - low
        pl.semaphore_signal(barrier, 1, device_id={"fsdp": mirror}, device_id_type=MESH)
    z_signals = even_n + (1 if low_n == 4 else 0)

    loads = [
        pltpu.make_async_copy(ref, stage.at[:, a], local_sem.at[a]) for a, ref in enumerate((q, k, v))
    ]
    load_w = pltpu.make_async_copy(w, w_v, local_sem.at[3])
    load_counts = pltpu.make_async_copy(counts, counts_v, local_sem.at[4])
    for load in (*loads, load_w, load_counts):
        load.start()

    load_w.wait()
    shard_tiles = w_st.shape[0]
    split = shard_tiles // 2 if y_n == x_n else shard_tiles
    x_cols = pl.ds(pl.multiple_of((x_at + x_n * core) * 128, 128), 128)
    y_cols = pl.ds(pl.multiple_of((y_at + x_n * core) * 128, 128), 128)
    kinds = [(0, split, x_cols)] + ([(split, shard_tiles, y_cols)] if split < shard_tiles else [])
    for first, last, at in kinds:
        part = w_v[first * 8 : last * 8, at].astype(F32)
        w_st[first:last] = part.reshape(last - first, 8, 128).astype(BF16)
    for load in loads:
        load.wait()
    pl.semaphore_wait(barrier, nb - 1 + z_signals)

    def send_qkv(g):
        cols = cols_of(g)
        pltpu.make_async_copy(stage.at[me, :, :, cols], qkv.at[me, :, :, cols], r_qkv.at[g]).start()

        @pl.loop(1, nb)
        def _(i):
            peer = lax.rem(me + i, nb)
            remote(
                stage.at[peer, :, :, cols], qkv.at[me, :, :, cols], s_qkv, r_qkv.at[g], {"bal": peer}
            ).start()

    send_qkv(0)
    pltpu.make_async_copy(w_st, wz.at[high, low], r_wf).start()
    for i in range(1, high_n):
        remote(w_st, wz.at[high, low], s_wf, r_wf, {"fsdp": far(i)}).start()
    pltpu.make_async_copy(cot.at[me], cot_v.at[me], r_cot).start()

    @pl.loop(1, nb)
    def _(i):
        peer = lax.rem(me + i, nb)
        remote(cot.at[peer], cot_v.at[me], s_cot, r_cot, {"bal": peer}).start()

    for g in range(1, GROUPS):
        send_qkv(g)

    load_counts.wait()

    my_counts = counts_v[pl.ds(me, 1), :].astype(F32)
    spread = lax.broadcasted_iota(jnp.int32, (rows, nb), 0) // 8 == lax.broadcasted_iota(
        jnp.int32, (rows, nb), 1
    )
    picked = jnp.where(spread, jnp.broadcast_to(my_counts, (rows, nb)), 0.0)
    row_count = jnp.sum(picked, axis=1, keepdims=True)
    slot = (lax.broadcasted_iota(jnp.int32, (rows, 1), 0) % 8).astype(F32)
    row_live = slot < row_count
    gather = (
        lax.broadcasted_iota(jnp.int32, (nb, rows), 1) // 8 == lax.broadcasted_iota(jnp.int32, (nb, rows), 0)
    )
    col_count = lax.dot_general(
        jnp.broadcast_to(my_counts, (8, nb)).astype(BF16),
        jnp.where(gather, 1.0, 0.0).astype(BF16),
        (((1,), (0,)), ((), ())),
        preferred_element_type=F32,
    )[0:1, :]
    col_slot = (lax.broadcasted_iota(jnp.int32, (1, rows), 1) % 8).astype(F32)
    col_live = col_slot < col_count
    scale = HEAD_DIM ** (-0.5)
    half_rows = features // 2
    plane_rows = half_rows // 2

    await_bytes(cot_v, r_cot)
    cot_2d = flat_rows(cot_v[...])
    step_rows = min(256, features)

    @pl.loop(0, features // step_rows)
    def _(n):
        shape = (step_rows, features)
        m = lax.broadcasted_iota(jnp.int32, shape, 0) + n * step_rows
        f = lax.broadcasted_iota(jnp.int32, shape, 1)
        z_of = (m % even_n) * 2 + (m // (even_n * chips)) % 2
        source = z_of * nb + ((m // even_n) % chips) * 2 + m // (nz * chips)
        chosen = jnp.where(f == source, 1.0, 0.0).astype(BF16)
        out = lax.dot_general(chosen, cot_2d, (((1,), (1,)), ((), ())), preferred_element_type=F32)
        cot_p[pl.ds(pl.multiple_of(n * step_rows, step_rows), step_rows), :] = out.astype(BF16)

    def attend(g):
        cols = cols_of(g)
        await_bytes(qkv.at[:, :, :, cols], r_qkv.at[g])

        for h in range(heads_per):
            head = pl.ds(pl.multiple_of(g * group_cols + h * HEAD_DIM, HEAD_DIM), HEAD_DIM)
            qh = flat_rows(qkv[:, 0, :, head])
            kh = flat_rows(qkv[:, 1, :, head])
            vh = flat_rows(qkv[:, 2, :, head])
            scores = lax.dot_general(qh, kh, (((1,), (1,)), ((), ())), preferred_element_type=F32)
            scores = jnp.where(col_live, scores * scale, -1e30)
            peak = jnp.max(scores, axis=1, keepdims=True)
            expo = jnp.exp(scores - peak)
            total = jnp.sum(expo, axis=1, keepdims=True)
            probs = (expo * (1.0 / total)).astype(BF16)
            out = lax.dot_general(probs, vh, (((1,), (0,)), ((), ())), preferred_element_type=F32)
            out = jnp.where(row_live, out, 0.0)
            out = out.astype(BF16)
            att_2d[:, head] = out
            att_s[:, :, head] = out.astype(F32).reshape(nb, 8, HEAD_DIM).astype(BF16)

    def share(g):
        cols = cols_of(g)
        a2 = att_2d[:, cols]
        their_rows = pl.ds(pl.multiple_of((1 - core) * half_rows, half_rows), half_rows)
        pair_s[g] = jnp.dot(cot_p[their_rows, :], a2, preferred_element_type=F32).astype(BF16)
        remote(pair_s.at[g], pair_r.at[g], s_pair, r_pair.at[g], sibling).start()
        my_rows = pl.ds(pl.multiple_of(core * half_rows, half_rows), half_rows)
        mine[g] = jnp.dot(cot_p[my_rows, :], a2, preferred_element_type=F32)

    def next_plane(g):
        await_bytes(pair_r.at[g], r_pair.at[g])
        theirs = pl.ds(pl.multiple_of((1 - parity) * plane_rows, plane_rows), plane_rows)
        two_s[g] = (mine[g, theirs, :] + pair_r[g, theirs, :].astype(F32)).astype(BF16)
        remote(two_s.at[g], two_r.at[g], s_two, r_two.at[g], next_z).start()
        ours = pl.ds(pl.multiple_of(parity * plane_rows, plane_rows), plane_rows)
        kept[g] = mine[g, ours, :] + pair_r[g, ours, :].astype(F32)

    def scatter(g):
        await_bytes(two_r.at[g], r_two.at[g])
        both = kept[g] + two_r[g].astype(F32)
        rs_s[g] = both.reshape(chips, even_n, group_cols).astype(BF16)
        pltpu.make_async_copy(rs_s.at[g, chip], rs_r.at[g, chip], r_rs.at[g]).start()

        @pl.loop(1, chips)
        def _(i):
            peer = lax.rem(chip + i, chips)
            remote(
                rs_s.at[g, peer], rs_r.at[g, chip], s_rs, r_rs.at[g], {"bal": peer * 2 + core}
            ).start()

    @pl.loop(0, GROUPS + 2)
    def _(t):
        @pl.when(t < GROUPS)
        def _():
            attend(t)
            share(t)

        @pl.when(jnp.logical_and(t >= 1, t < GROUPS + 1))
        def _():
            next_plane(t - 1)

        @pl.when(t >= 2)
        def _():
            scatter(t - 2)

        @pl.when(t == 0)
        def _():
            await_bytes(wz.at[:, low], r_wf)
            for i in range(1, low_n):
                remote(wz.at[:, low], wz.at[:, low], s_wn, r_wn, {"fsdp": near(i)}).start()

        @pl.when(t == 2)
        def _():
            await_bytes(wz.at[:, pl.ds(0, low_n - 1)], r_wn)
            for kind, (first, last, at) in enumerate(kinds):
                tiles = pl.ds(first, last - first)
                have = wz.at[:, :, tiles]
                place = wfull.at[:, :, tiles, :, at]
                pltpu.make_async_copy(have, place, r_wa).start()
                for i in range(1, x_n):
                    if kind == 0:
                        peer = (y_at * x_n + lax.rem(x_at + i, x_n)) * 2 + core
                    else:
                        peer = (lax.rem(y_at + i, y_n) * x_n + x_at) * 2 + core
                    remote(have, place, s_wa, r_wa, {"bal": peer}).start()

    for g in range(GROUPS):
        await_bytes(rs_r.at[g], r_rs.at[g])
        plane = jnp.sum(rs_r[g].astype(F32), axis=0)
        for t in range(group_cols // 128):
            z_32[pl.ds(g * (group_cols // 128) + t, even_n, stride=8), :] = plane[:, t * 128 : (t + 1) * 128]
    z_s[...] = z_32[...].reshape(z_s.shape).astype(BF16)
    pltpu.make_async_copy(z_s.at[z_half], z_r.at[z_half], r_z).start()

    @pl.loop(0, even_n - 1)
    def _(i):
        peer = lax.rem(z_half + far_first(i, even_n), even_n)
        remote(z_s.at[peer], z_r.at[z_half], s_z, r_z, {"fsdp": peer * 2 + parity}).start()

    pltpu.make_async_copy(att_s.at[me], att_h.at[me], r_att).start()

    @pl.loop(1, nb)
    def _(i):
        peer = lax.rem(me + i, nb)
        remote(att_s.at[peer], att_h.at[me], s_att, r_att, {"bal": peer}).start()

    my_half = wfull.at[:, :, :, :, pl.ds(pl.multiple_of(core * half_width, half_width), half_width)]
    await_bytes(my_half, r_wa)
    remote(my_half, my_half, s_sib, r_sib, sibling).start()

    await_bytes(z_r, r_z)
    row_s[...] = jnp.sum(z_r[...].astype(F32), axis=0)
    pltpu.make_async_copy(row_s, row_r.at[me], r_row).start()

    @pl.loop(1, nb)
    def _(i):
        peer = lax.rem(me + i, nb)
        remote(row_s, row_r.at[me], s_row, r_row, {"bal": peer}).start()

    await_bytes(my_half, r_sib)
    await_bytes(att_h, r_att)
    att_2d[...] = flat_rows(att_h[...])
    blocks = 2 if high_n % 2 == 0 else 1
    out_cols = blocks * low_n * nb

    @pl.loop(0, high_n // blocks)
    def _(n):
        wn = wfull[pl.ds(n * blocks, blocks)].astype(F32).reshape(out_cols, width).astype(BF16)
        out = lax.dot_general(att_2d[...], wn, (((1,), (1,)), ((), ())), preferred_element_type=F32)
        out_at = pl.ds(pl.multiple_of(n * out_cols, out_cols), out_cols)
        mixed_v[:, :, out_at] = out.reshape(nb, 8, out_cols).astype(BF16)

    store_mixed = pltpu.make_async_copy(mixed_v, mixed_out, out_sem.at[0])
    store_mixed.start()

    await_bytes(row_r, r_row)
    for t in range(8):
        grad_v[:, t * 128 : (t + 1) * 128] = row_r[:, t, :]
    store_grad = pltpu.make_async_copy(grad_v, grad_out, out_sem.at[1])
    store_grad.start()

    await_bytes(qkv.at[pl.ds(0, nb - 1)], s_qkv)
    await_bytes(att_s.at[pl.ds(0, nb - 1)], s_att)
    await_bytes(cot_v.at[pl.ds(0, nb - 1)], s_cot)
    await_bytes(wz.at[pl.ds(0, high_n - 1), 0], s_wf)
    await_bytes(wz.at[:, pl.ds(0, low_n - 1)], s_wn)
    await_bytes(wfull.at[:, :, :, :, pl.ds(0, (x_n - 1) * 128)], s_wa)
    await_bytes(my_half, s_sib)
    await_bytes(pair_s, s_pair)
    await_bytes(rs_s.at[:, pl.ds(0, chips - 1)], s_rs)
    await_bytes(two_s, s_two)
    await_bytes(z_s.at[pl.ds(0, even_n - 1)], s_z)
    await_bytes(row_r.at[pl.ds(0, nb - 1)], s_row)
    store_mixed.wait()
    store_grad.wait()


def local(nz, nb, query_rows, key_rows, value_rows, cotangent, out_weight, token_counts):
    cells, genes, width = query_rows.shape
    shard = out_weight.shape[0]
    features = nz * shard
    rows = cells * genes
    group_cols = width // GROUPS
    chips = nb // 2
    low_n = min(4, nz // 2)
    high_n = nz // low_n
    vmem = pltpu.VMEM
    dma = pltpu.SemaphoreType.DMA
    scratch = [
        vmem((nb, 3, genes, width), BF16),
        vmem((nb, 3, genes, width), BF16),
        vmem((nb, genes, width), BF16),
        vmem((nb, genes, width), BF16),
        vmem((nb, genes, features), BF16),
        vmem((features, rows), BF16),
        vmem((shard, width), BF16),
        vmem((shard // 8, 8, 128), BF16),
        vmem((high_n, low_n, shard // 8, 8, 128), BF16),
        vmem((high_n, low_n, shard // 8, 8, width), BF16),
        vmem(token_counts.shape, jnp.int32),
        vmem((nb, genes, features), BF16),
        vmem((rows, width), BF16),
        vmem((GROUPS, features // 2, group_cols), F32),
        vmem((GROUPS, features // 2, group_cols), BF16),
        vmem((GROUPS, features // 2, group_cols), BF16),
        vmem((GROUPS, features // 4, group_cols), F32),
        vmem((GROUPS, features // 4, group_cols), BF16),
        vmem((GROUPS, features // 4, group_cols), BF16),
        vmem((GROUPS, chips, nz // 2, group_cols), BF16),
        vmem((GROUPS, chips, nz // 2, group_cols), BF16),
        vmem((nz * 4, 128), F32),
        vmem((nz // 2, 8, 128), BF16),
        vmem((nz // 2, 8, 128), BF16),
        vmem((8, 128), F32),
        vmem((nb, 8, 128), F32),
        vmem((shard, width), F32),
        dma, dma((GROUPS,)),
        dma, dma,
        dma, dma,
        dma, dma,
        dma, dma,
        dma, dma,
        dma, dma,
        dma, dma((GROUPS,)),
        dma, dma((GROUPS,)),
        dma, dma((GROUPS,)),
        dma, dma,
        dma, dma,
        dma((5,)),
        dma((2,)),
    ]
    operands = (query_rows, key_rows, value_rows, cotangent, out_weight, token_counts)
    any_spec = pl.BlockSpec(memory_space=pl.ANY)
    return pl.pallas_call(
        functools.partial(kernel, nz, nb),
        out_shape=(
            jax.ShapeDtypeStruct((cells, genes, features), BF16),
            jax.ShapeDtypeStruct((shard, width), F32),
        ),
        in_specs=[any_spec] * 6,
        out_specs=(any_spec, any_spec),
        scratch_shapes=scratch,
        compiler_params=pltpu.CompilerParams(
            collective_id=0, has_side_effects=True, vmem_limit_bytes=48 * 1024 * 1024
        ),
        name="attend_project",
    )(*[pltpu.with_memory_space_constraint(a, pltpu.HBM) for a in operands])


def solution(mesh):
    nz, nb = mesh.shape["fsdp"], mesh.shape["bal"]
    placed = (
        P("fsdp", "bal", None),
        P("fsdp", "bal", None),
        P("fsdp", "bal", None),
        P("fsdp", "bal", None),
        P("fsdp", None),
        P("fsdp", None),
    )
    return jax.shard_map(
        functools.partial(local, nz, nb),
        mesh=mesh,
        in_specs=placed,
        out_specs=(P("fsdp", "bal", None), P("fsdp", None)),
        check_vma=False,
    )
```

time: 91.1 us -> 89.8 us (0.986)
  Pallas kernels: 88.9 us -> 87.5 us
    pallas_call x1, Pallas kernels: 88.9 us -> 87.5 us  [local(): pl.pallas_call(functools.partial(kernel, nz, nb), out_shape=(jax.ShapeDty...]
where the time goes in v3:
time: 89.8 us; the launch traced here: 89.6 us
  Pallas kernels  87.5 us (97%)
  local copies, waits for them, and re-layouts  1.45 us (2%)
    pallas_call x1, Pallas kernels, local(): pl.pallas_call(functools.partial(kernel, nz, nb), out_shape=(jax.ShapeDty...  87.5 us

profile of v3, /device:TPU:1, one launch (start us, length us, event | category | flops | bytes accessed | tf_op | source)
XLA Modules:
  0.0 89.6 jit_solution(16355616584332745992)
XLA Ops:
  0.6 87.5 %attend_project.1 = (bf16[32,8,1024]{2,1,0:T(8,128)(2,1)S(1)}, f32[32,1024]{1,0:T(8,128)S(1)}) custom-call(bf16[32,8,1024]{2,1,0:T(8,128)(2,1)} %q.1, bf16[32,8,1024]{2,1,0:T(8,128)(2,1)} %k.1, bf16[32,8,1024]{2,1,0:T(8,128)(2,1)} %v.1, bf16[32,8,1024]{2,1,0:T(8,128)(2,1)} %cot.1, bf16[32,1024]{1,0:T(8,128)(2,1)} %w.1, s32[32,32]{1,0:T(8,128)} %counts.1), custom_call_target="tpu_custom_call" | custom-call | tf_op jit(solution)/shard_map/attend_project/pallas_call | solution.py:393
  88.2 0.8 copy.10
  88.9 0.7 copy.11

commit v4 on v3

--- a/solution.py
+++ b/solution.py
@@ -190,9 +190,9 @@
             peak = jnp.max(scores, axis=1, keepdims=True)
             expo = jnp.exp(scores - peak)
             total = jnp.sum(expo, axis=1, keepdims=True)
-            probs = (expo * (1.0 / total)).astype(BF16)
+            probs = expo.astype(BF16)
             out = lax.dot_general(probs, vh, (((1,), (0,)), ((), ())), preferred_element_type=F32)
-            out = jnp.where(row_live, out, 0.0)
+            out = jnp.where(row_live, out * (1.0 / total), 0.0)
             out = out.astype(BF16)
             att_2d[:, head] = out
             att_s[:, :, head] = out.astype(F32).reshape(nb, 8, HEAD_DIM).astype(BF16)

time: 89.8 us -> 89.6 us (level)
  no operation moved by 1% of the time
where the time goes in v4:
time: 89.6 us; the launch traced here: 89.4 us
  Pallas kernels  87.3 us (97%)
  local copies, waits for them, and re-layouts  1.45 us (2%)
    pallas_call x1, Pallas kernels, local(): pl.pallas_call(functools.partial(kernel, nz, nb), out_shape=(jax.ShapeDty...  87.3 us

profile of v4, /device:TPU:1, one launch (start us, length us, event | category | flops | bytes accessed | tf_op | source)
XLA Modules:
  0.0 89.4 jit_solution(17167784171387087478)
XLA Ops:
  0.6 87.3 %attend_project.1 = (bf16[32,8,1024]{2,1,0:T(8,128)(2,1)S(1)}, f32[32,1024]{1,0:T(8,128)S(1)}) custom-call(bf16[32,8,1024]{2,1,0:T(8,128)(2,1)} %q.1, bf16[32,8,1024]{2,1,0:T(8,128)(2,1)} %k.1, bf16[32,8,1024]{2,1,0:T(8,128)(2,1)} %v.1, bf16[32,8,1024]{2,1,0:T(8,128)(2,1)} %cot.1, bf16[32,1024]{1,0:T(8,128)(2,1)} %w.1, s32[32,32]{1,0:T(8,128)} %counts.1), custom_call_target="tpu_custom_call" | custom-call | tf_op jit(solution)/shard_map/attend_project/pallas_call | solution.py:393
  88.0 0.8 copy.10
  88.8 0.7 copy.11
